TPU v7x, 256 devices: a whole 4x4x8 slice. The times are simulated.
256 devices in a mesh: loop: 4 (over y_hi, core), inner: 64 (over z, x, y_lo).
Axes of the slice: x: 4, y: 4 (y_hi: 2, y_lo: 2; y = y_hi * 2 + y_lo), z: 8, core: 2. Of those that a mesh axis runs over, the one named last changes fastest.
Arguments:
- snapshots: bfloat16 [65536, 1024], P(('loop', 'inner')), may hold values from -6 to 6
- bins: int32 [65536], replicated, may hold values from 0 to 511, as said below
- pairs: int32 [2048, 2], replicated, may hold values from 0 to 511, as said below
- start_weights: bfloat16 [1024, 32], replicated, may hold values from -0.1875 to 0.1875
Outputs:
- basis: float32 [65536, 96], P(('loop', 'inner'))
- coefficients: float32 [4, 32, 32], replicated
Inputs may be any that keep to these rules, and one draw needn't show every extreme that they name: `bins`: the snapshot in row n has a bin in [r * 8, (r + 1) * 8), where r = (n // 256) mod (64). `pairs`: every row (a, b) has a <= b <= a + 8; every bin is paired with itself.
All inputs are finite; a program needn't handle non-finite values.
Results may differ from a plain program's by a relative error of at most 0.0003.
Values may be sent and summed in bfloat16 or wider, within the bound.
A program may use at most 64 MiB of HBM per device.

v0:
```python
import jax
import jax.numpy as jnp
from jax import lax
from jax.sharding import PartitionSpec as P

STEPS = 2
BINS_COL = 8


def extended(cells, sides, width):
    for axis, dim in sides:
        count = lax.axis_size(axis)
        ends = count - 1
        head = lax.slice_in_dim(cells, 0, width, axis=dim)
        tail = lax.slice_in_dim(cells, cells.shape[dim] - width, cells.shape[dim], axis=dim)
        cells = jnp.concatenate(
            [
                lax.ppermute(tail, axis, [(i, (i + 1) % count) for i in range(ends)]),
                cells,
                lax.ppermute(head, axis, [((i + 1) % count, i) for i in range(ends)]),
            ],
            axis=dim,
        )
    return cells


def matches(values, targets):
    return (values[:, None] == targets[None, :]).astype(jnp.float32)


def local_gram(left, right):
    return jnp.dot(left.T, right, precision=lax.Precision.HIGHEST)


def finish(matrix, gram_total):
    lower_factor = jnp.linalg.cholesky(gram_total)
    result = lax.linalg.triangular_solve(
        lower_factor, matrix, left_side=False, lower=True, transpose_a=True
    )
    return (result, lower_factor.T)


def local(snapshots, bins, pairs, start_weights):
    row_count, features = snapshots.shape
    block_width = start_weights.shape[1]
    n_loop = lax.axis_size("loop")
    n_inner = lax.axis_size("inner")
    column = lax.axis_index("inner")
    group = lax.axis_index("loop")
    bin_grid = jnp.pad(
        bins.reshape(n_loop, n_inner, row_count), ((0, 0), (1, 1), (0, 0)), constant_values=-1
    )
    stacked = lax.all_gather(snapshots[None], "loop", axis=0, tiled=True)
    partner_rows = extended(stacked, (("inner", 1),), row_count)
    tile_rows = partner_rows.reshape(n_loop * 3 * row_count, features)
    tile_bins = lax.dynamic_slice_in_dim(bin_grid, column, 3, 1).reshape(-1)
    my_bins = lax.dynamic_slice_in_dim(bins, (group * n_inner + column) * row_count, row_count)
    bin_base = column * BINS_COL
    my_ids = bin_base + jnp.arange(BINS_COL, dtype=jnp.int32)
    window_ids = bin_base - BINS_COL + jnp.arange(3 * BINS_COL, dtype=jnp.int32)
    left_bins = pairs[:, 0]
    right_bins = pairs[:, 1]
    pair_count = jnp.dot(
        matches(left_bins, my_ids).T,
        matches(right_bins, window_ids),
        precision=lax.Precision.HIGHEST,
    )
    pair_count = pair_count + jnp.dot(
        matches(right_bins, my_ids).T,
        matches(left_bins, window_ids),
        precision=lax.Precision.HIGHEST,
    )
    linked_bins = jnp.where(pair_count > 0.5, 1.0, 0.0).astype(jnp.float32)
    my_hot = matches(my_bins, my_ids)
    row_links = jnp.dot(my_hot, linked_bins)
    mine_wide = snapshots.astype(jnp.float32)
    mine_norms = jnp.sum(mine_wide * mine_wide, axis=1)
    epsilon = features / 3.0
    part_hot = matches(tile_bins, window_ids) * (tile_bins >= 0).astype(jnp.float32)[:, None]
    band_mask = jnp.dot(row_links, part_hot.T)
    part_wide = tile_rows.astype(jnp.float32)
    part_norms = jnp.sum(part_wide * part_wide, axis=1)
    products = lax.dot_general(
        snapshots, tile_rows, (((1,), (1,)), ((), ())), preferred_element_type=jnp.float32
    )
    distance = mine_norms[:, None] + part_norms[None, :] - 2.0 * products
    kept_tiles = [band_mask * jnp.exp(-distance / epsilon)]

    def current_kernel(which):
        return kept_tiles[which]

    degree = jnp.sum(current_kernel(0), axis=1)
    inv_root = lax.rsqrt(degree)
    start_block = jnp.dot(snapshots, start_weights, preferred_element_type=jnp.float32)
    start_total = lax.psum(local_gram(start_block, start_block), ("loop", "inner"))
    current, unused = finish(start_block, start_total)
    basis_blocks = [current]
    coefficients = []
    previous = current
    prev_b = jnp.zeros((block_width, block_width), jnp.float32)
    for lanczos_step in range(STEPS):
        scaled = inv_root[:, None] * current
        vec_stack = lax.all_gather(scaled[None], "loop", axis=0, tiled=True)
        vec_strip = extended(vec_stack, (("inner", 1),), row_count)
        strip = vec_strip.reshape(n_loop * 3 * row_count, block_width)
        total = jnp.dot(current_kernel(0), strip, precision=lax.Precision.HIGHEST)
        image = inv_root[:, None] * total
        projected = lax.psum(local_gram(current, image), ("loop", "inner"))
        image = image - jnp.dot(current, projected, precision=lax.Precision.HIGHEST)
        if lanczos_step > 0:
            image = image - jnp.dot(previous, prev_b.T, precision=lax.Precision.HIGHEST)
        gram_total = lax.psum(local_gram(image, image), ("loop", "inner"))
        following, factor = finish(image, gram_total)
        coefficients.append(projected)
        coefficients.append(factor)
        previous = current
        prev_b = factor
        current = following
        basis_blocks.append(current)
    return (jnp.concatenate(basis_blocks, axis=1), jnp.stack(coefficients))


def solution(mesh):
    in_specs = (P(("loop", "inner"), None), P(), P(), P())
    out_specs = (P(("loop", "inner"), None), P())
    return jax.shard_map(local, mesh=mesh, in_specs=in_specs, out_specs=out_specs, check_vma=False)
```

profile of v0, /device:TPU:1, one launch (start us, length us, event | category | flops | bytes accessed | tf_op | source)
XLA Modules:
  0.0 579.3 jit_solution(10393950573843033094)
XLA Ops:
  11.2 90.2 %psum.35 = f32[32,32]{0,1:T(8,128)S(1)} all-reduce(f32[32,32]{0,1:T(8,128)S(1)} %fusion.50), channel_id=1, replica_groups=mesh['loop'=4,'inner'=64] {'loop','inner'}, use_global_device_ids=true, to_apply=%region_0.1 | all-reduce | flops 1024 | bytes 8192 | tf_op jit(solution)/shard_map/psum | solution.py:95
  102.8 5.3 collective-permute-start
  108.1 2.9 cholesky.59
  112.4 2.4 custom-call.7
  118.8 31.0 %collective-permute-done.1 = bf16[4,256,1024]{2,1,0:T(8,128)(2,1)S(1)} collective-permute-done((bf16[4,256,1024]{2,1,0:T(8,128)(2,1)}, bf16[4,256,1024]{2,1,0:T(8,128)(2,1)S(1)}, u32[]{:S(2)}, u32[]{:S(2)}) %collective-permute-start.1) | collective-permute-done | bytes 2097184 | tf_op jit(solution)/shard_map/ppermute | solution.py:20
  149.8 44.7 %collective-permute-done = bf16[4,256,1024]{2,1,0:T(8,128)(2,1)} collective-permute-done((bf16[4,256,1024]{2,1,0:T(8,128)(2,1)}, bf16[4,256,1024]{2,1,0:T(8,128)(2,1)}, u32[]{:S(2)}, u32[]{:S(2)}) %collective-permute-start) | collective-permute-done | bytes 2097184 | tf_op jit(solution)/shard_map/ppermute | solution.py:18
  194.5 3.6 multiply_reduce_fusion
  198.2 3.5 fusion
  201.7 3.1 fusion.46
  205.0 7.2 %all-gather.1 = f32[1024,32]{0,1:T(8,128)S(1)} all-gather(f32[256,32]{0,1:T(8,128)S(1)} %get-tuple-element.20), channel_id=3, replica_groups=mesh['loop'=4,'inner'=64] {'loop'}, dimensions={0}, use_global_device_ids=true | all-gather | bytes 163840 | tf_op jit(solution)/shard_map/all_gather | solution.py:103
  213.6 4.8 collective-permute-start.2
  220.2 3.2 collective-permute-done.2
  223.6 2.8 convolution_multiply_fusion.3
  226.5 80.3 %psum.36 = f32[32,32]{0,1:T(8,128)S(1)} all-reduce(f32[32,32]{0,1:T(8,128)S(1)} %fusion.51), channel_id=1, replica_groups=mesh['loop'=4,'inner'=64] {'loop','inner'}, use_global_device_ids=true, to_apply=%region_6.9 | all-reduce | flops 1024 | bytes 8192 | tf_op jit(solution)/shard_map/psum | solution.py:108
  307.2 75.5 %psum.37 = f32[32,32]{0,1:T(8,128)S(1)} all-reduce(f32[32,32]{0,1:T(8,128)S(1)} %fusion.52), channel_id=1, replica_groups=mesh['loop'=4,'inner'=64] {'loop','inner'}, use_global_device_ids=true, to_apply=%region_7.10 | all-reduce | flops 1024 | bytes 8192 | tf_op jit(solution)/shard_map/psum | solution.py:112
  382.8 2.9 cholesky.70
  390.3 7.4 %all-gather.2 = f32[1024,32]{0,1:T(8,128)S(1)} all-gather(f32[256,32]{0,1:T(8,128)S(1)} %get-tuple-element.22), channel_id=4, replica_groups=mesh['loop'=4,'inner'=64] {'loop'}, dimensions={0}, use_global_device_ids=true | all-gather | bytes 163840 | tf_op jit(solution)/shard_map/all_gather | solution.py:103
  399.1 4.0 collective-permute-start.4
  404.7 2.6 collective-permute-done.4
  407.5 3.5 convolution_multiply_fusion.2
  411.1 76.5 %psum.38 = f32[32,32]{0,1:T(8,128)S(1)} all-reduce(f32[32,32]{0,1:T(8,128)S(1)} %fusion.53), channel_id=1, replica_groups=mesh['loop'=4,'inner'=64] {'loop','inner'}, use_global_device_ids=true, to_apply=%region_8.11 | all-reduce | flops 1024 | bytes 8192 | tf_op jit(solution)/shard_map/psum | solution.py:108
  488.7 75.3 %psum.39 = f32[32,32]{0,1:T(8,128)S(1)} all-reduce(f32[32,32]{0,1:T(8,128)S(1)} %fusion.54), channel_id=1, replica_groups=mesh['loop'=4,'inner'=64] {'loop','inner'}, use_global_device_ids=true, to_apply=%region_9.12 | all-reduce | flops 1024 | bytes 8192 | tf_op jit(solution)/shard_map/psum | solution.py:112
  564.1 2.9 cholesky.81
  568.4 2.4 custom-call.9
  (70 shorter events, 26.8 us)
Async XLA Ops:
  7.2 2.6 copy-start
  7.2 94.4 %all-gather.5.cloned.1.call-start = ((), (), s32[]{:S(2)}) async-start(), calls=%async_computation | async-start | bytes 2621440 | tf_op jit(solution)/shard_map/all_gather | solution.py:53
  101.5 48.3 %collective-permute-start.1 = (bf16[4,256,1024]{2,1,0:T(8,128)(2,1)}, bf16[4,256,1024]{2,1,0:T(8,128)(2,1)S(1)}, u32[]{:S(2)}, u32[]{:S(2)}) collective-permute-start(bf16[4,256,1024]{2,1,0:T(8,128)(2,1)} %bitcast.93), channel_id=1, source_target_pairs={{1,0},{2,1},{3,2},{4,3},{5,4},{6,5},{7,6},{8,7},{9,8},{10,9},{11,1... | collective-permute-start | bytes 6291464 | tf_op jit(solution)/shard_map/ppermute | solution.py:20
  102.8 91.7 %collective-permute-start = (bf16[4,256,1024]{2,1,0:T(8,128)(2,1)}, bf16[4,256,1024]{2,1,0:T(8,128)(2,1)}, u32[]{:S(2)}, u32[]{:S(2)}) collective-permute-start(bf16[4,256,1024]{2,1,0:T(8,128)(2,1)} %bitcast.94), channel_id=1, source_target_pairs={{0,1},{1,2},{2,3},{3,4},{4,5},{5,6},{6,7},{7,8},{8,9},{9,10},{10,1... | collective-permute-start | bytes 6291464 | tf_op jit(solution)/shard_map/ppermute | solution.py:18
  118.8 79.3 %copy-start.1 = (bf16[256,1024]{1,0:T(8,128)(2,1)S(1)}, bf16[256,1024]{1,0:T(8,128)(2,1)}, u32[]{:S(2)}) copy-start(bf16[256,1024]{1,0:T(8,128)(2,1)} %param.7) | copy-start | bytes 1572868
  204.8 185.5 %copy-start.5 = (f32[256]{0:T(256)}, f32[256]{0:T(256)S(1)}, u32[]{:S(2)}) copy-start(f32[256]{0:T(256)S(1)} %rsqrt.7) | copy-start | bytes 3076
  212.3 7.9 %collective-permute-start.3 = (f32[4,256,32]{1,0,2:T(4,128)S(1)}, f32[4,256,32]{1,0,2:T(4,128)S(1)}, u32[]{:S(2)}, u32[]{:S(2)}) collective-permute-start(f32[4,256,32]{1,0,2:T(4,128)S(1)} %reshape.60), channel_id=1, source_target_pairs={{1,0},{2,1},{3,2},{4,3},{5,4},{6,5},{7,6},{8,7},{9,8},{10,9},{11,1... | collective-permute-start | bytes 393224 | tf_op jit(solution)/shard_map/ppermute | solution.py:20
  213.6 9.8 %collective-permute-start.2 = (f32[4,256,32]{1,0,2:T(4,128)S(1)}, f32[4,256,32]{1,0,2:T(4,128)S(1)}, u32[]{:S(2)}, u32[]{:S(2)}) collective-permute-start(f32[4,256,32]{1,0,2:T(4,128)S(1)} %reshape.60), channel_id=1, source_target_pairs={{0,1},{1,2},{2,3},{3,4},{4,5},{5,6},{6,7},{7,8},{8,9},{9,10},{10,1... | collective-permute-start | bytes 393224 | tf_op jit(solution)/shard_map/ppermute | solution.py:18
  306.9 83.4 %copy-start.2 = (f32[32,32]{0,1:T(8,128)}, f32[32,32]{0,1:T(8,128)S(1)}, u32[]{:S(2)}) copy-start(f32[32,32]{0,1:T(8,128)S(1)} %psum.36) | copy-start | bytes 12292
  397.8 173.9 %copy-start.3 = (f32[32,32]{0,1:T(8,128)S(1)}, f32[32,32]{0,1:T(8,128)}, u32[]{:S(2)}) copy-start(f32[32,32]{0,1:T(8,128)} %copy-done.2) | copy-start | bytes 12292
  397.8 173.9 %copy-start.4 = (f32[1,32,32]{1,2,0:T(8,128)S(1)}, f32[1,32,32]{1,2,0:T(8,128)}, u32[]{:S(2)}) copy-start(f32[1,32,32]{1,2,0:T(8,128)} %get-tuple-element.12) | copy-start | bytes 12292
  397.8 6.8 %collective-permute-start.5 = (f32[4,256,32]{1,0,2:T(4,128)S(1)}, f32[4,256,32]{1,0,2:T(4,128)S(1)}, u32[]{:S(2)}, u32[]{:S(2)}) collective-permute-start(f32[4,256,32]{1,0,2:T(4,128)S(1)} %reshape.61), channel_id=1, source_target_pairs={{1,0},{2,1},{3,2},{4,3},{5,4},{6,5},{7,6},{8,7},{9,8},{10,9},{11,1... | collective-permute-start | bytes 393224 | tf_op jit(solution)/shard_map/ppermute | solution.py:20
  399.1 8.2 %collective-permute-start.4 = (f32[4,256,32]{1,0,2:T(4,128)S(1)}, f32[4,256,32]{1,0,2:T(4,128)S(1)}, u32[]{:S(2)}, u32[]{:S(2)}) collective-permute-start(f32[4,256,32]{1,0,2:T(4,128)S(1)} %reshape.61), channel_id=1, source_target_pairs={{0,1},{1,2},{2,3},{3,4},{4,5},{5,6},{6,7},{7,8},{8,9},{9,10},{10,1... | collective-permute-start | bytes 393224 | tf_op jit(solution)/shard_map/ppermute | solution.py:18
Sparse Core Ops, SparseCore 0:
  9.8 33.8 all-gather.4
where the time goes:
time: 581 us; the launch traced here: 579 us
  blocking collectives  413 us (71%)
  waiting for transfers between devices  85.5 us (15%)
  other arithmetic  26.3 us (5%)
  matrix products  18.7 us (3%)
  starting transfers between devices  17.9 us (3%)
  between operations  14.3 us (2%)
    psum x2, blocking collectives, local(): projected = lax.psum(local_gram(current, image), ('loop', 'inner'))  157 us
    psum x2, blocking collectives, local(): gram_total = lax.psum(local_gram(image, image), ('loop', 'inner'))  151 us
    psum x1, blocking collectives, local(): lax.psum(local_gram(start_block, start_block), ('loop', 'inner'))  90.2 us
    ppermute x3, waiting for transfers between devices, extended(): lax.ppermute(tail, axis, [(i, (i + 1) % count) for i in range(ends)])  50.5 us
    ppermute x3, waiting for transfers between devices, extended(): lax.ppermute(head, axis, [((i + 1) % count, i) for i in range(ends)])  34.4 us
    all_gather x2, blocking collectives, local(): vec_stack = lax.all_gather(scaled[None], 'loop', axis=0, tiled=True)  14.7 us
    ppermute x3, starting transfers between devices, extended(): lax.ppermute(tail, axis, [(i, (i + 1) % count) for i in range(ends)])  14 us
  transfers between devices with their start and end apart: 7, of which 6 were waited for; matrix products, arithmetic and copies ran while one was open for 2% of the time, Pallas kernels for 0%

commit v1 on v0

--- a/solution.py
+++ b/solution.py
@@ -105,7 +105,7 @@
         strip = vec_strip.reshape(n_loop * 3 * row_count, block_width)
         total = jnp.dot(current_kernel(0), strip, precision=lax.Precision.HIGHEST)
         image = inv_root[:, None] * total
-        projected = lax.psum(local_gram(current, image), ("loop", "inner"))
+        projected = lax.psum(lax.psum(local_gram(current, image), "loop"), "inner")
         image = image - jnp.dot(current, projected, precision=lax.Precision.HIGHEST)
         if lanczos_step > 0:
             image = image - jnp.dot(previous, prev_b.T, precision=lax.Precision.HIGHEST)

time: 581 us -> 1060 us (1.82)
  blocking collectives: 413 us -> 896 us
    psum x2 -> x4, blocking collectives: 157 us -> 529 us  [local(): projected = lax.psum(lax.psum(local_gram(current, image), 'loop'), 'inner')]
    psum x2, blocking collectives: 151 us -> 262 us  [local(): gram_total = lax.psum(local_gram(image, image), ('loop', 'inner'))]
  transfers between devices with their start and end apart: 7 -> 7, of which waited for: 6 -> 6; matrix products, arithmetic and copies ran while one was open for 2% -> 1% of each run, Pallas kernels for 0% -> 0%
where the time goes in v1:
time: 1060 us
  blocking collectives  896 us (85%)
  waiting for transfers between devices  86.2 us (8%)
  other arithmetic  26.3 us (2%)
  matrix products  18.7 us (2%)
  starting transfers between devices  17.9 us (2%)
  between operations  14.3 us (1%)
    psum x4, blocking collectives, local(): projected = lax.psum(lax.psum(local_gram(current, image), 'loop'), 'inner')  529 us
    psum x2, blocking collectives, local(): gram_total = lax.psum(local_gram(image, image), ('loop', 'inner'))  262 us
    psum x1, blocking collectives, local(): lax.psum(local_gram(start_block, start_block), ('loop', 'inner'))  90.2 us
    ppermute x3, waiting for transfers between devices, extended(): lax.ppermute(tail, axis, [(i, (i + 1) % count) for i in range(ends)])  51.1 us
    ppermute x3, waiting for transfers between devices, extended(): lax.ppermute(head, axis, [((i + 1) % count, i) for i in range(ends)])  34.4 us
  transfers between devices with their start and end apart: 7, of which 6 were waited for; matrix products, arithmetic and copies ran while one was open for 1% of the time, Pallas kernels for 0%

profile of v1, /device:TPU:1, one launch (start us, length us, event | category | flops | bytes accessed | tf_op | source)
XLA Modules:
  0.0 1063.0 jit_solution(16362513395534886772)
XLA Ops:
  11.2 90.2 %psum.49 = f32[32,32]{0,1:T(8,128)S(1)} all-reduce(f32[32,32]{0,1:T(8,128)S(1)} %fusion.50), channel_id=1, replica_groups=mesh['loop'=4,'inner'=64] {'loop','inner'}, use_global_device_ids=true, to_apply=%region_0.1 | all-reduce | flops 1024 | bytes 8192 | tf_op jit(solution)/shard_map/psum | solution.py:95
  102.8 5.3 collective-permute-start
  108.1 2.9 cholesky.59
  118.8 31.0 %collective-permute-done.1 = bf16[4,256,1024]{2,1,0:T(8,128)(2,1)S(1)} collective-permute-done((bf16[4,256,1024]{2,1,0:T(8,128)(2,1)}, bf16[4,256,1024]{2,1,0:T(8,128)(2,1)S(1)}, u32[]{:S(2)}, u32[]{:S(2)}) %collective-permute-start.1) | collective-permute-done | bytes 2097184 | tf_op jit(solution)/shard_map/ppermute | solution.py:20
  149.8 44.7 %collective-permute-done = bf16[4,256,1024]{2,1,0:T(8,128)(2,1)} collective-permute-done((bf16[4,256,1024]{2,1,0:T(8,128)(2,1)}, bf16[4,256,1024]{2,1,0:T(8,128)(2,1)}, u32[]{:S(2)}, u32[]{:S(2)}) %collective-permute-start) | collective-permute-done | bytes 2097184 | tf_op jit(solution)/shard_map/ppermute | solution.py:18
  194.5 3.6 multiply_reduce_fusion
  198.2 3.5 fusion
  201.7 3.1 fusion.46
  205.0 7.2 all-gather.1
  213.6 4.8 collective-permute-start.2
  220.2 3.2 collective-permute-done.2
  223.6 2.8 convolution_multiply_fusion.3
  226.5 12.5 %psum.50 = f32[32,32]{0,1:T(8,128)S(1)} all-reduce(f32[32,32]{0,1:T(8,128)S(1)} %fusion.51), channel_id=1, replica_groups=mesh['loop'=4,'inner'=64] {'loop'}, use_global_device_ids=true, to_apply=%region_6.9 | all-reduce | flops 1024 | bytes 8192 | tf_op jit(solution)/shard_map/psum | solution.py:108
  239.1 251.1 %psum.51 = f32[32,32]{0,1:T(8,128)S(1)} all-reduce(f32[32,32]{0,1:T(8,128)S(1)} %psum.50), channel_id=1, replica_groups=mesh['loop'=4,'inner'=64] {'inner'}, use_global_device_ids=true, to_apply=%region_7.10 | all-reduce | flops 1024 | bytes 8192 | tf_op jit(solution)/shard_map/psum | solution.py:108
  490.5 132.1 %psum.52 = f32[32,32]{0,1:T(8,128)S(1)} all-reduce(f32[32,32]{0,1:T(8,128)S(1)} %fusion.52), channel_id=1, replica_groups=mesh['loop'=4,'inner'=64] {'loop','inner'}, use_global_device_ids=true, to_apply=%region_8.11 | all-reduce | flops 1024 | bytes 8192 | tf_op jit(solution)/shard_map/psum | solution.py:112
  622.6 2.9 cholesky.70
  630.1 7.4 all-gather.2
  638.9 4.0 collective-permute-start.4
  644.4 3.3 collective-permute-done.4
  647.8 3.5 convolution_multiply_fusion.2
  651.5 12.5 %psum.53 = f32[32,32]{0,1:T(8,128)S(1)} all-reduce(f32[32,32]{0,1:T(8,128)S(1)} %fusion.53), channel_id=1, replica_groups=mesh['loop'=4,'inner'=64] {'loop'}, use_global_device_ids=true, to_apply=%region_9.12 | all-reduce | flops 1024 | bytes 8192 | tf_op jit(solution)/shard_map/psum | solution.py:108
  664.0 252.7 %psum.54 = f32[32,32]{0,1:T(8,128)S(1)} all-reduce(f32[32,32]{0,1:T(8,128)S(1)} %psum.53), channel_id=1, replica_groups=mesh['loop'=4,'inner'=64] {'inner'}, use_global_device_ids=true, to_apply=%region_10.13 | all-reduce | flops 1024 | bytes 8192 | tf_op jit(solution)/shard_map/psum | solution.py:108
  917.9 129.9 %psum.55 = f32[32,32]{0,1:T(8,128)S(1)} all-reduce(f32[32,32]{0,1:T(8,128)S(1)} %fusion.54), channel_id=1, replica_groups=mesh['loop'=4,'inner'=64] {'loop','inner'}, use_global_device_ids=true, to_apply=%region_11.14 | all-reduce | flops 1024 | bytes 8192 | tf_op jit(solution)/shard_map/psum | solution.py:112
  1047.8 2.9 cholesky.81
  (72 shorter events, 31.6 us)
Async XLA Ops:
  7.2 2.6 copy-start
  7.2 94.4 %all-gather.5.cloned.1.call-start = ((), (), s32[]{:S(2)}) async-start(), calls=%async_computation | async-start | bytes 2621440 | tf_op jit(solution)/shard_map/all_gather | solution.py:53
  101.5 48.3 %collective-permute-start.1 = (bf16[4,256,1024]{2,1,0:T(8,128)(2,1)}, bf16[4,256,1024]{2,1,0:T(8,128)(2,1)S(1)}, u32[]{:S(2)}, u32[]{:S(2)}) collective-permute-start(bf16[4,256,1024]{2,1,0:T(8,128)(2,1)} %bitcast.93), channel_id=1, source_target_pairs={{1,0},{2,1},{3,2},{4,3},{5,4},{6,5},{7,6},{8,7},{9,8},{10,9},{11,1... | collective-permute-start | bytes 6291464 | tf_op jit(solution)/shard_map/ppermute | solution.py:20
  102.8 91.7 %collective-permute-start = (bf16[4,256,1024]{2,1,0:T(8,128)(2,1)}, bf16[4,256,1024]{2,1,0:T(8,128)(2,1)}, u32[]{:S(2)}, u32[]{:S(2)}) collective-permute-start(bf16[4,256,1024]{2,1,0:T(8,128)(2,1)} %bitcast.94), channel_id=1, source_target_pairs={{0,1},{1,2},{2,3},{3,4},{4,5},{5,6},{6,7},{7,8},{8,9},{9,10},{10,1... | collective-permute-start | bytes 6291464 | tf_op jit(solution)/shard_map/ppermute | solution.py:18
  118.8 79.3 %copy-start.1 = (bf16[256,1024]{1,0:T(8,128)(2,1)S(1)}, bf16[256,1024]{1,0:T(8,128)(2,1)}, u32[]{:S(2)}) copy-start(bf16[256,1024]{1,0:T(8,128)(2,1)} %param.7) | copy-start | bytes 1572868
  204.8 425.3 %copy-start.5 = (f32[256]{0:T(256)}, f32[256]{0:T(256)S(1)}, u32[]{:S(2)}) copy-start(f32[256]{0:T(256)S(1)} %rsqrt.7) | copy-start | bytes 3076
  212.3 7.9 collective-permute-start.3
  213.6 9.8 collective-permute-start.2
  490.1 139.9 %copy-start.2 = (f32[32,32]{0,1:T(8,128)}, f32[32,32]{0,1:T(8,128)S(1)}, u32[]{:S(2)}) copy-start(f32[32,32]{0,1:T(8,128)S(1)} %psum.51) | copy-start | bytes 12292
  637.6 417.8 %copy-start.3 = (f32[32,32]{0,1:T(8,128)S(1)}, f32[32,32]{0,1:T(8,128)}, u32[]{:S(2)}) copy-start(f32[32,32]{0,1:T(8,128)} %copy-done.2) | copy-start | bytes 12292
  637.6 417.8 %copy-start.4 = (f32[1,32,32]{1,2,0:T(8,128)S(1)}, f32[1,32,32]{1,2,0:T(8,128)}, u32[]{:S(2)}) copy-start(f32[1,32,32]{1,2,0:T(8,128)} %get-tuple-element.12) | copy-start | bytes 12292
  637.6 6.8 collective-permute-start.5
  638.9 8.8 collective-permute-start.4
Sparse Core Ops, SparseCore 0:
  9.8 33.8 all-gather.4
